TPU v7x, 256 devices: a whole 4x4x8 slice. The times are simulated.
256 devices in a mesh: front: 8 (over z), row: 4 (over y), col: 8 (over x, core).
Axes of the slice: x: 4, y: 4, z: 8, core: 2. Of those that a mesh axis runs over, the one named last changes fastest.
Arguments:
- front_entries: float32 [16384, 16384], P(('front', 'row'), 'col'), as said below
- child_updates: float32 [8, 4096, 4096], P('front', ('row', 'col')), as said below
- block_offsets: int32 [8, 32], replicated, may hold values from 0 to 127, as said below
- block_counts: int32 [8], replicated, may hold values from 16 to 32, as said below
Outputs:
- trailing: float32 [16384, 16384], P(('front', 'row'), 'col')
- panel_factor: float32 [16384, 1024], P(('front', 'row'))
Inputs may be any that keep to these rules, and one draw needn't show every extreme that they name: `block_offsets`: within one child all offsets differ. Block a of a child maps to a parent block i with (i // 4) % 4 == a // 8. For each child and each of its 4 groups of 8 consecutive blocks, at most 2 blocks map to parent blocks with the same i // 16, and exactly 2 for some value in every group. `block_counts`: one child has all 32 blocks live. `front_entries`: Symmetric. The leading block, rows and columns below 1024, has all eigenvalues at least 0.6 * 2 * 512, diagonal entries in 0.6 * 2 * 512 to 1.2 * 2 * 512, and off-diagonal entries of magnitude below 0.4 * 2 * 512. Entries with exactly one index below 1024 lie in -2 to 2; where neither is, off-diagonal entries lie in -1 to 1 and diagonal entries in 2 to 6. `child_updates`: each child's block is symmetric with entries of magnitude below 0.5 / 8.
All inputs are finite; a program needn't handle non-finite values.
Results may differ from a plain program's by a relative error of at most 0.0001.
Values sent between devices are 32-bit elements; how exact they have to be, the bound alone decides.
No kernel may reach another device: no remote copies, remote signals or barrier semaphores. Data moves between devices by JAX's collectives and lax.ppermute only.
A program may use at most 128 MiB of HBM per device.

v0:
```python
import jax
import jax.numpy as jnp
from jax import lax
from jax.sharding import PartitionSpec as P

S = 4096
BLOCK = 128
PANEL = 512
PANELS = 2


HIGHEST = lax.Precision.HIGHEST


def spread(x, axis, root):
    mine = lax.axis_index(axis) == root
    return lax.psum(jnp.where(mine, x, jnp.zeros_like(x)), axis)


def count_before(labels):
    length = labels.shape[-1]
    positions = jnp.arange(length)
    same_label = labels[..., :, None] == labels[..., None, :]
    earlier = positions[None, :] < positions[:, None]
    return jnp.sum(same_label & earlier, axis=-1)


def slot_table(labels, ranking, label_count, slot_count):
    label_ids = jnp.arange(label_count)[:, None, None]
    slot_ids = jnp.arange(slot_count)[None, :, None]
    matches = (labels[None, None, :] == label_ids) & (ranking[None, None, :] == slot_ids)
    element = jnp.arange(labels.shape[-1])[None, None, :]
    picked = jnp.sum(jnp.where(matches, element, 0), axis=-1)
    present = jnp.any(matches, axis=-1)
    return (picked.reshape(-1), present.reshape(-1))


def on_device(front_entries, child_updates, block_offsets, block_counts):
    front_count = lax.axis_size("front")
    row_count = lax.axis_size("row")
    col_count = lax.axis_size("col")
    own_rows, own_cols = front_entries.shape
    child_rows = child_updates.shape[1]
    child_blocks = S // BLOCK
    owned_blocks = own_rows // BLOCK
    grouping = front_count // col_count
    row_blocks = S // (BLOCK * row_count)
    col_slots = 2 * grouping * row_count
    col_span = own_cols // BLOCK
    front_index = lax.axis_index("front")
    row_index = lax.axis_index("row")
    col_index = lax.axis_index("col")
    parent_front = block_offsets // (owned_blocks * row_count)
    parent_col = parent_front // grouping
    col_rank = count_before(parent_col)
    my_col = lax.dynamic_index_in_dim(parent_col, front_index, 0, keepdims=False)
    my_col_rank = lax.dynamic_index_in_dim(col_rank, front_index, 0, keepdims=False)
    my_fronts = lax.dynamic_index_in_dim(parent_front, front_index, 0, keepdims=False)
    my_count = lax.dynamic_index_in_dim(block_counts, front_index, 0, keepdims=False)
    picked, present = slot_table(my_col, my_col_rank, col_count, col_slots)
    block_live = jnp.arange(child_blocks) < my_count
    present = present & jnp.take(block_live, picked)
    first_row = lax.axis_index(("row", "col")) * child_rows
    row_live = (first_row + jnp.arange(child_rows)) // BLOCK < my_count
    blocks = child_updates[0].reshape(child_rows, child_blocks, BLOCK)
    chosen = jnp.take(blocks, picked, axis=1)
    chosen = jnp.where(present[None, :, None] & row_live[:, None, None], chosen, 0.0)
    outgoing = chosen.reshape(child_rows, col_count * col_slots * BLOCK)
    by_columns = lax.all_to_all(outgoing, "col", split_axis=1, concat_axis=0, tiled=True)
    group_fronts = lax.dynamic_slice_in_dim(my_fronts, row_index * row_blocks, row_blocks, 0)
    group_rank = count_before(group_fronts)
    picked_rows, present_rows = slot_table(group_fronts, group_rank, front_count, 2)
    row_view = by_columns.reshape(row_blocks, BLOCK, col_slots * BLOCK)
    sending = jnp.take(row_view, picked_rows, axis=0)
    sending = jnp.where(present_rows[:, None, None], sending, 0.0)
    sending = sending.reshape(front_count * 2 * BLOCK, col_slots * BLOCK)
    arrived = lax.all_to_all(sending, "front", split_axis=0, concat_axis=0, tiled=True)
    arrived = arrived.reshape(front_count, 2, BLOCK, col_slots, BLOCK)
    all_group = lax.dynamic_slice_in_dim(parent_front, row_index * row_blocks, row_blocks, 1)
    all_rank = count_before(all_group)
    all_slot = lax.dynamic_slice_in_dim(
        block_offsets % owned_blocks, row_index * row_blocks, row_blocks, 1
    )
    row_select = (
        (all_group == front_index)[:, None, None, :]
        & (all_rank[:, None, None, :] == jnp.arange(2)[None, :, None, None])
        & (all_slot[:, None, None, :] == jnp.arange(owned_blocks)[None, None, :, None])
    )
    row_select = jnp.any(row_select, axis=-1).astype(jnp.float32)
    col_select = (
        (parent_col == col_index)[:, None, None, :]
        & (col_rank[:, None, None, :] == jnp.arange(col_slots)[None, :, None, None])
        & (
            (block_offsets % col_span)[:, None, None, :]
            == jnp.arange(col_span)[None, None, :, None]
        )
    )
    col_select = jnp.any(col_select, axis=-1).astype(jnp.float32)
    gathered_rows = jnp.einsum("gcs,gcxkb->gsxkb", row_select, arrived, precision=HIGHEST)
    contribution = jnp.einsum("gsxkb,gku->sxub", gathered_rows, col_select, precision=HIGHEST)
    assembled = front_entries + contribution.reshape(own_rows, own_cols)
    global_rows = lax.axis_index(("front", "row")) * own_rows + jnp.arange(own_rows)
    global_cols = col_index * own_cols + jnp.arange(own_cols)
    columns_list = []
    for panel_no in range(PANELS):
        panel_start = panel_no * PANEL
        panel_cols = spread(assembled[:, panel_start : panel_start + PANEL], "col", 0)
        owner_row = panel_start // own_rows
        offset_rows = panel_start % own_rows
        diagonal = spread(panel_cols, ("front", "row"), owner_row)
        factor = jnp.linalg.cholesky(diagonal)
        identity = jnp.eye(PANEL, dtype=jnp.float32)
        inverse = jax.scipy.linalg.solve_triangular(factor, identity, lower=True)
        panel_range = jnp.arange(PANEL)[None, :]
        column = jnp.dot(
            panel_cols, inverse.T, precision=HIGHEST, preferred_element_type=jnp.float32
        )
        column = jnp.where(global_rows[:, None] - panel_start >= panel_range, column, 0.0)
        columns_list.append(column)
        span_groups = own_cols // own_rows
        pieces = [
            spread(column, ("front", "row"), col_index * span_groups + member)
            for member in range(span_groups)
        ]
        across = jnp.concatenate(pieces, axis=0)
        assembled = assembled - jnp.dot(
            column, across.T, precision=HIGHEST, preferred_element_type=jnp.float32
        )
    panel_factor = jnp.concatenate(columns_list, axis=1)
    retained = (global_rows >= PANELS * PANEL)[:, None] & (global_cols >= PANELS * PANEL)[None, :]
    trailing = jnp.where(retained, assembled, 0.0)
    return (trailing, panel_factor)


def solution(mesh):
    placed = (P(("front", "row"), "col"), P("front", ("row", "col"), None), P(), P())
    return jax.shard_map(
        on_device,
        mesh=mesh,
        in_specs=placed,
        out_specs=(P(("front", "row"), "col"), P(("front", "row"), None)),
        check_vma=False,
    )
```

profile of v0, /device:TPU:32, one launch (start us, length us, event | category | flops | bytes accessed | tf_op | source)
XLA Modules:
  0.0 1450.8 jit_solution(9458514656477227775)
XLA Ops:
  14.9 2.9 copy.60
  19.7 2.8 gather_fusion.1
  22.5 5.6 copy.62
  28.1 5.3 copy.63
  33.6 5.3 select_select_fusion
  38.9 4.6 all-to-all-start
  44.4 48.8 %all-to-all-done = f32[128,8,1024]{2,0,1:T(8,128)} async-done(((f32[128,8,1024]{2,0,1:T(8,128)}), f32[128,8,1024]{2,0,1:T(8,128)}, u32[]{:S(2)}, u32[]{:S(2)}) %all-to-all-start) | async-done | bytes 4194336 | tf_op jit(solution)/shard_map/all_to_all | solution.py:69
  93.2 6.5 gather_fusion.2
  99.7 5.9 fusion.2
  105.6 8.7 all-to-all-start.1
  115.6 5.3 copy.70
  122.2 176.6 %all-to-all-done.1 = f32[8,256,1024]{2,1,0:T(8,128)} async-done(((f32[8,256,1024]{2,1,0:T(8,128)}), f32[8,256,1024]{2,1,0:T(8,128)}, u32[]{:S(2)}, u32[]{:S(2)}) %all-to-all-start.1) | async-done | bytes 8388640 | tf_op jit(solution)/shard_map/all_to_all | solution.py:77
  298.8 5.5 copy.85
  304.3 22.3 %fusion.3 = f32[8,4,128,8,128]{4,1,3,2,0:T(4,128)S(1)} fusion(pred[8,2,4,1,1]{2,1,4,3,0:T(4,128)(4,1)S(1)} %copy.77, f32[8,2,128,8,128]{4,3,2,1,0:T(8,128)S(1)} %bitcast.148), kind=kOutput, calls=%fused_computation.11 | convolution fusion | flops 100663296 | bytes 25165888 | tf_op jit(solution)/shard_map/gcs,gcxkb->gsxkb/dot_general | solution.py:99
  326.6 5.9 fusion
  332.5 3.9 copy.92
  336.4 5.3 copy.84
  341.8 6.5 add.231
  350.6 63.5 %all-reduce.10.cloned.1.call-done = f32[512,512]{0,1:T(8,128)} async-done(((f32[512,512]{0,1:T(8,128)}), f32[512,512]{0,1:T(8,128)}) %all-reduce.10.cloned.1.call-update) | async-done | bytes 1048592 | tf_op jit(solution)/shard_map/psum | solution.py:17
  415.7 150.5 %all-reduce.12.cloned.1.call-done = f32[512,512]{0,1:T(8,128)} async-done(((f32[512,512]{0,1:T(8,128)}), f32[512,512]{0,1:T(8,128)}) %all-reduce.12.cloned.1.call-update) | async-done | bytes 1048592 | tf_op jit(solution)/shard_map/psum | solution.py:17
  569.2 11.7 cholesky.286
  581.0 9.8 custom-call.27
  591.5 11.7 cholesky.305
  604.6 10.2 custom-call.28
  615.5 11.7 cholesky.326
  627.9 9.8 custom-call.29
  638.3 11.7 cholesky.343
  654.5 11.7 while.4
  666.2 39.3 %custom-call.30 = f32[4,128,128]{1,2,0:T(8,128)S(1)} custom-call(f32[4,128,128]{2,1,0:T(8,128)S(1)} %get-tuple-element.18), custom_call_target="InvertDiagBlocksLowerTriangular" | custom-call | tf_op jit(solution)/shard_map/jit(_solve_triangular)/triangular_solve | solution.py:113
  711.4 4.2 broadcast_select_fusion.8
  715.7 162.0 %all-reduce.20.cloned.1.call-done = (f32[512,512]{0,1:T(8,128)}, f32[512,512]{0,1:T(8,128)}, f32[512,512]{0,1:T(8,128)}, f32[512,512]{0,1:T(8,128)}) async-done(((f32[512,512]{0,1:T(8,128)}, f32[512,512]{0,1:T(8,128)}, f32[512,512]{0,1:T(8,128)}, f32[512,512]{0,1:T(8,128)}), (f32[512,512]{0,1:T(8,128)}, f32[512,512]{0,1:T(8,128)}, f32[512,512]{0,1:T(8,128)}, ...) | async-done | bytes 4194320 | tf_op jit(solution)/shard_map/psum | solution.py:17
  877.7 10.0 fusion.23
  890.9 65.6 %all-reduce.14.cloned.1.call-done = f32[512,512]{0,1:T(8,128)} async-done(((f32[512,512]{0,1:T(8,128)}), f32[512,512]{0,1:T(8,128)}) %all-reduce.14.cloned.1.call-update) | async-done | bytes 1048592 | tf_op jit(solution)/shard_map/psum | solution.py:17
  957.9 150.8 %all-reduce.16.cloned.1.call-done = f32[512,512]{0,1:T(8,128)} async-done(((f32[512,512]{0,1:T(8,128)}), f32[512,512]{0,1:T(8,128)}) %all-reduce.16.cloned.1.call-update) | async-done | bytes 1048592 | tf_op jit(solution)/shard_map/psum | solution.py:17
  1112.7 11.7 cholesky.358
  1124.6 9.8 custom-call.31
  1136.9 11.7 cholesky.377
  1150.0 10.2 custom-call.32
  1161.9 11.7 cholesky.398
  1174.3 9.8 custom-call.33
  1185.5 11.7 cholesky.415
  1201.6 11.9 while.5
  1214.2 40.1 %custom-call.34 = f32[4,128,128]{1,2,0:T(8,128)S(1)} custom-call(f32[4,128,128]{2,1,0:T(8,128)} %copy-done.4), custom_call_target="InvertDiagBlocksLowerTriangular" | custom-call | tf_op jit(solution)/shard_map/jit(_solve_triangular)/triangular_solve | solution.py:113
  1260.2 4.2 broadcast_select_fusion.3
  1266.0 2.9 copy.76
  1268.9 157.7 %all-reduce.18.cloned.1.call-done = (f32[512,512]{0,1:T(8,128)}, f32[512,512]{0,1:T(8,128)}, f32[512,512]{0,1:T(8,128)}, f32[512,512]{0,1:T(8,128)}) async-done(((f32[512,512]{0,1:T(8,128)}, f32[512,512]{0,1:T(8,128)}, f32[512,512]{0,1:T(8,128)}, f32[512,512]{0,1:T(8,128)}), (f32[512,512]{0,1:T(8,128)}, f32[512,512]{0,1:T(8,128)}, f32[512,512]{0,1:T(8,128)}, ...) | async-done | bytes 4194320 | tf_op jit(solution)/shard_map/psum | solution.py:17
  1426.6 11.8 subtract_select_fusion
  1438.4 5.3 copy.75
  (166 shorter events, 80.8 us)
Async XLA Ops:
  38.9 54.3 %all-to-all-start = ((f32[128,8,1024]{2,0,1:T(8,128)}), f32[128,8,1024]{2,0,1:T(8,128)}, u32[]{:S(2)}, u32[]{:S(2)}) async-start(f32[128,8,1024]{2,0,1:T(8,128)} %select_select_fusion), calls=%async_computation | async-start | bytes 8388608 | tf_op jit(solution)/shard_map/all_to_all | solution.py:69
  105.6 9.2 copy-start.5
  105.6 193.2 %all-to-all-start.1 = ((f32[8,256,1024]{2,1,0:T(8,128)}), f32[8,256,1024]{2,1,0:T(8,128)}, u32[]{:S(2)}, u32[]{:S(2)}) async-start(f32[8,256,1024]{2,1,0:T(8,128)} %fusion.2), calls=%async_computation.1 | async-start | bytes 16777216 | tf_op jit(solution)/shard_map/all_to_all | solution.py:77
  114.3 299.8 %all-reduce.10.cloned.1.call-start = ((), (), s32[]{:S(2)}) async-start(), calls=%async_computation.2 | async-start | bytes 2097152 | tf_op jit(solution)/shard_map/psum | solution.py:17
  350.6 215.6 %all-reduce.12.cloned.1.call-start = ((), (), s32[]{:S(2)}) async-start(), calls=%async_computation.3 | async-start | bytes 2097152 | tf_op jit(solution)/shard_map/psum | solution.py:17
  415.2 462.5 %all-reduce.20.cloned.1.call-start = ((), (), s32[]{:S(2)}) async-start(), calls=%async_computation.7 | async-start | bytes 8388608 | tf_op jit(solution)/shard_map/psum | solution.py:17
  653.4 58.0 %copy-start.1 = (f32[512,512]{0,1:T(8,128)S(1)}, f32[512,512]{0,1:T(8,128)}, u32[]{:S(2)}) copy-start(f32[512,512]{0,1:T(8,128)} %all-reduce.10.cloned.1.call-done) | copy-start | bytes 3145732
  715.6 240.9 %all-reduce.14.cloned.1.call-start = ((), (), s32[]{:S(2)}) async-start(), calls=%async_computation.4 | async-start | bytes 2097152 | tf_op jit(solution)/shard_map/psum | solution.py:17
  887.7 2.0 copy-start
  890.8 217.9 %all-reduce.16.cloned.1.call-start = ((), (), s32[]{:S(2)}) async-start(), calls=%async_computation.5 | async-start | bytes 2097152 | tf_op jit(solution)/shard_map/psum | solution.py:17
  957.6 469.0 %all-reduce.18.cloned.1.call-start = ((), (), s32[]{:S(2)}) async-start(), calls=%async_computation.6 | async-start | bytes 8388608 | tf_op jit(solution)/shard_map/psum | solution.py:17
  1111.7 1.0 copy-start.3
  1201.6 58.6 %copy-start.2 = (f32[512,512]{0,1:T(8,128)S(1)}, f32[512,512]{0,1:T(8,128)}, u32[]{:S(2)}) copy-start(f32[512,512]{0,1:T(8,128)} %all-reduce.14.cloned.1.call-done) | copy-start | bytes 3145732
  1213.5 0.7 copy-start.4
Sparse Core Ops, SparseCore 0:
  350.7 63.4 all-reduce.9
  418.2 147.9 all-reduce.11
  715.7 161.9 all-reduce.19
  891.0 65.5 all-reduce.13
  960.8 147.9 all-reduce.15
  1264.6 161.9 all-reduce.17
where the time goes:
time: 1460 us; the launch traced here: 1450 us
  waiting for transfers between devices  976 us (67%)
  other arithmetic  274 us (19%)
  local copies, waits for them, and re-layouts  89.1 us (6%)
  matrix products  77.4 us (5%)
  between operations  20.2 us (1%)
    psum x6, waiting for transfers between devices, spread(): return lax.psum(jnp.where(mine, x, jnp.zeros_like(x)), axis)  750 us
    all_to_all x1, waiting for transfers between devices, on_device(): lax.all_to_all(sending, 'front', split_axis=0, concat_axis=0, tiled=True)  177 us
    another operation x30, other arithmetic, on_device(): factor = jnp.linalg.cholesky(diagonal)  159 us
    another operation x5, other arithmetic, on_device(): inverse = jax.scipy.linalg.solve_triangular(factor, identity, lower=True)  81.6 us
    all_to_all x1, waiting for transfers between devices, on_device(): lax.all_to_all(outgoing, 'col', split_axis=1, concat_axis=0, tiled=True)  48.8 us
    unnamed x18, local copies, waits for them, and re-layouts  29.5 us
  transfers between devices with their start and end apart: 8, of which 8 were waited for; matrix products, arithmetic and copies ran while one was open for 1% of the time, Pallas kernels for 0%

commit v1 on v0

v1 whole, which is shorter than its diff:
```python
import functools

import jax
import jax.numpy as jnp
from jax import lax
from jax.experimental import pallas as pl
from jax.experimental.pallas import tpu as pltpu
from jax.sharding import PartitionSpec as P

BLOCK = 128
LEAD = 8
LEADING = LEAD * BLOCK
HIGHEST = lax.Precision.HIGHEST
NN = (((1,), (0,)), ((), ()))
NT = (((1,), (1,)), ((), ()))
TN = (((0,), (0,)), ((), ()))
F32 = jnp.float32
SMEM = pl.BlockSpec(memory_space=pltpu.SMEM)
VMEM = pl.BlockSpec(memory_space=pltpu.VMEM)
ANY = pl.BlockSpec(memory_space=pl.ANY)


def mm(a, b, dims):
    return lax.dot_general(a, b, dims, precision=HIGHEST, preferred_element_type=F32)


def split(x):
    high = x.astype(jnp.bfloat16)
    low = (x - high.astype(F32)).astype(jnp.bfloat16)
    return high, low


def mm3(a, b, dims):
    ah, al = a
    bh, bl = b
    dot = functools.partial(lax.dot_general, dimension_numbers=dims, preferred_element_type=F32)
    return dot(ah, bh) + (dot(al, bh) + dot(ah, bl))


def call(body, name, out_shape, in_specs, out_specs, scratch=(), flops=0, moved=0, **more):
    return pl.pallas_call(
        body,
        name=name,
        out_shape=out_shape,
        in_specs=in_specs,
        out_specs=out_specs,
        scratch_shapes=list(scratch),
        compiler_params=pltpu.CompilerParams(vmem_limit_bytes=48 << 20),
        cost_estimate=pl.CostEstimate(flops=flops, bytes_accessed=moved, transcendentals=0),
        **more,
    )


def shape(*dims):
    return jax.ShapeDtypeStruct(dims, F32)


def lead_columns_body(off, cnt, child, out):
    g = lax.axis_index("front")
    own = lax.axis_index("row") * lax.axis_size("col") + lax.axis_index("col")
    out[...] = jnp.zeros_like(out)
    live = cnt[g]
    for b in range(off.shape[1]):
        o = off[g, b]

        @pl.when((o < LEAD) & (b < live) & (own < live))
        def _():
            out[o] = child[0, :, b * BLOCK : (b + 1) * BLOCK]


def lead_rows_body(per_front, off, cnt, got, corner, panel):
    g = lax.axis_index("front")
    r = lax.axis_index("row")
    rows = got.shape[0]
    corner[...] = jnp.zeros_like(corner)
    panel[...] = jnp.zeros_like(panel)
    for j in range(rows):
        o = off[g, r * rows + j]
        f = o // per_front
        rank = jnp.int32(0)
        for i in range(j):
            rank += (off[g, r * rows + i] // per_front == f).astype(jnp.int32)

        panel[f, rank] = got[j]

        @pl.when(o < LEAD)
        def _():
            for q in range(corner.shape[0]):
                corner[q, rank] = got[j]


def gather_rows_body(per_front, to_front, off, cnt, got, base, out):
    r = lax.axis_index("row")
    f = 0 if to_front else lax.axis_index("front")
    children = got.shape[0]
    rows = off.shape[1] // lax.axis_size("row")
    owned = out.shape[0] // BLOCK
    out[...] = base[...]

    def child(g, carry):
        rank = jnp.int32(0)
        for j in range(rows):
            a = r * rows + j
            o = off[g, a]
            hit = o // per_front == f

            @pl.when(hit & (a < cnt[g]))
            def _():
                at = pl.multiple_of((o % owned) * BLOCK, BLOCK)
                out[pl.ds(at, BLOCK), :] += got[g, rank]

            rank += hit.astype(jnp.int32)
        return carry

    lax.fori_loop(0, children, child, 0)


def far_columns_body(per_col, off, cnt, child, out, sems, slots):
    g = lax.axis_index("front")
    groups = out.shape[0]
    blocks = off.shape[1]
    for c in range(groups):
        slots[c] = 0
    copies = []
    for b in range(blocks):
        o = off[g, b]
        c = o // per_col
        use = (o >= LEAD) & (b < cnt[g])
        k = jnp.minimum(slots[c], out.shape[1] - 1)
        copy = pltpu.make_async_copy(
            child.at[0, :, pl.ds(b * BLOCK, BLOCK)], out.at[c, k], sems.at[b]
        )
        copies.append((use, copy))

        @pl.when(use)
        def _():
            copy.start()
            slots[c] = k + 1

    for use, copy in copies:

        @pl.when(use)
        def _():
            copy.wait()


def far_rows_body(per_front, off, cnt, got, out, sems):
    g = lax.axis_index("front")
    r = lax.axis_index("row")
    rows = got.shape[0]
    copies = []
    for j in range(rows):
        a = r * rows + j
        o = off[g, a]
        f = o // per_front
        rank = jnp.int32(0)
        for i in range(j):
            rank += (off[g, r * rows + i] // per_front == f).astype(jnp.int32)
        use = (o >= LEAD) & (a < cnt[g])
        copy = pltpu.make_async_copy(got.at[j], out.at[f, jnp.minimum(rank, 1)], sems.at[j])
        copies.append((use, copy))

        @pl.when(use)
        def _():
            copy.start()

    for use, copy in copies:

        @pl.when(use)
        def _():
            copy.wait()


def factor_block(w):
    sub = lax.broadcasted_iota(jnp.int32, (8, BLOCK), 0)
    for lo in range(0, BLOCK, 8):
        r0 = w[lo : lo + 8, 0:BLOCK]
        r1 = w[lo : lo + 8, BLOCK : 2 * BLOCK]
        e = [jnp.broadcast_to(r0[:, lo + k : lo + k + 1], (8, BLOCK)) for k in range(8)]
        recip, across, top0, top1 = [], {}, [], []
        pivots = jnp.ones((8, BLOCK), F32)
        for i in range(8):
            row = {k: jnp.broadcast_to(e[k][i : i + 1, :], (8, BLOCK)) for k in range(i, 8)}
            inv = 1.0 / row[i]
            recip.append(inv)
            m = jnp.where(sub > i, e[i] * inv, 0.0)
            b0 = jnp.broadcast_to(r0[i : i + 1, :], (8, BLOCK))
            b1 = jnp.broadcast_to(r1[i : i + 1, :], (8, BLOCK))
            top0.append(b0)
            top1.append(b1)
            for k in range(i + 1, 8):
                across[i, k] = row[k]
                e[k] = e[k] - m * row[k]
            r0 = r0 - m * b0
            r1 = r1 - m * b1
            pivots = jnp.where(sub == i, row[i], pivots)
        scale = lax.rsqrt(pivots)
        w[lo : lo + 8, 0:BLOCK] = r0 * scale
        w[lo : lo + 8, BLOCK : 2 * BLOCK] = r1 * scale
        q = lo + 8
        while q < BLOCK:
            n = min(32, BLOCK - q)

            def tall(x):
                return jnp.concatenate([x] * (n // 8), axis=0) if n > 8 else x

            g0 = w[q : q + n, 0:BLOCK]
            g1 = w[q : q + n, BLOCK : 2 * BLOCK]
            e = [jnp.broadcast_to(g0[:, lo + k : lo + k + 1], (n, BLOCK)) for k in range(8)]
            for i in range(8):
                m = e[i] * tall(recip[i])
                for k in range(i + 1, 8):
                    e[k] = e[k] - m * tall(across[i, k])
                g0 = g0 - m * tall(top0[i])
                g1 = g1 - m * tall(top1[i])
            w[q : q + n, 0:BLOCK] = g0
            w[q : q + n, BLOCK : 2 * BLOCK] = g1
            q += n


def factor_body(a, u_ref, inv_ref, s, w):
    nb = a.shape[0]
    for c in range(nb):
        s[:, c * BLOCK : (c + 1) * BLOCK] = a[c]
    ri = lax.broadcasted_iota(jnp.int32, (BLOCK, BLOCK), 0)
    ci = lax.broadcasted_iota(jnp.int32, (BLOCK, BLOCK), 1)
    eye = (ri == ci).astype(F32)

    def step(k, carry):
        at = pl.ds(pl.multiple_of(k * BLOCK, BLOCK), BLOCK)
        w[:, 0:BLOCK] = s[at, at]
        w[:, BLOCK : 2 * BLOCK] = eye
        factor_block(w)
        inverse = jnp.where(ri >= ci, w[:, BLOCK : 2 * BLOCK], 0.0)
        inv_ref[at, :] = inverse
        u_ref[at, at] = jnp.where(ri <= ci, w[:, 0:BLOCK], 0.0)
        for kk in range(nb - 1):

            @pl.when(k == kk)
            def _():
                h = (kk + 1) * BLOCK
                u = mm(inverse, s[kk * BLOCK : h, h:], NN)
                u_ref[kk * BLOCK : h, h:] = u
                for i in range(kk + 1, nb):
                    o = (i - kk - 1) * BLOCK
                    s[i * BLOCK : (i + 1) * BLOCK, i * BLOCK :] -= mm(
                        u[:, o : o + BLOCK], u[:, o:], TN
                    )

        return carry

    lax.fori_loop(0, nb, step, 0)


def solve_body(u, inv, a, m_ref, t_ref, work):
    nb = a.shape[0]
    rows = a.shape[1]
    for c in range(nb):
        work[:, c * BLOCK : (c + 1) * BLOCK] = a[c]
    first = (lax.axis_index("front") * lax.axis_size("row") + lax.axis_index("row")) * rows
    ri = first + lax.broadcasted_iota(jnp.int32, (rows, BLOCK), 0)
    ci = lax.broadcasted_iota(jnp.int32, (rows, BLOCK), 1)
    for k in range(nb):
        at = slice(k * BLOCK, (k + 1) * BLOCK)
        m = mm(work[:, at], inv[at, :], NT)
        work[:, at] = m
        m_ref[:, at] = jnp.where(ri >= ci + k * BLOCK, m, 0.0)
        if k + 1 < nb:
            work[:, (k + 1) * BLOCK :] -= mm(m, u[at, (k + 1) * BLOCK :], NN)
    for k in reversed(range(nb)):
        at = slice(k * BLOCK, (k + 1) * BLOCK)
        x = work[:, at]
        if k + 1 < nb:
            x = x - mm(t_ref[:, (k + 1) * BLOCK :], u[at, (k + 1) * BLOCK :], NT)
        t_ref[:, at] = mm(x, inv[at, :], NN)


def final_body(per_front, per_col, off, cnt, t, pair, got, base, out):
    step = pl.program_id(0)
    f = lax.axis_index("front")
    r = lax.axis_index("row")
    c = lax.axis_index("col")
    rows = off.shape[1] // lax.axis_size("row")
    owned = out.shape[0] // BLOCK
    span = out.shape[1] // BLOCK
    width = 2 * BLOCK

    @pl.when(step == 0)
    def _():
        out[...] = base[...]

    for half in range(2):
        g = 2 * step + half
        rank = jnp.int32(0)
        for j in range(rows):
            a = r * rows + j
            o = off[g, a]
            hit = o // per_front == f
            at = pl.multiple_of((o % owned) * BLOCK, BLOCK)
            here = rank

            @pl.when(hit & (a < cnt[g]) & (o >= LEAD))
            def _():
                def column(b, k):
                    p = off[g, b]
                    use = (p // per_col == c) & (p >= LEAD) & (b < cnt[g])

                    @pl.when(use)
                    def _():
                        to = pl.multiple_of((p % span) * BLOCK, BLOCK)
                        out[pl.ds(at, BLOCK), pl.ds(to, BLOCK)] += got[half, here, k]

                    return k + use.astype(jnp.int32)

                lax.fori_loop(0, off.shape[1], column, jnp.int32(0))

            rank += hit.astype(jnp.int32)

    tt = split(t[:, pl.ds(pl.multiple_of(step * width, width), width)])
    chunk = 512
    for q in range(0, out.shape[1], chunk):
        other = jnp.concatenate([pair[0, q : q + chunk, :], pair[1, q : q + chunk, :]], axis=1)
        out[:, q : q + chunk] -= mm3(tt, split(other), NT)

    @pl.when(step == pl.num_programs(0) - 1)
    def _():
        top = f * lax.axis_size("row") + r

        @pl.when(top * out.shape[0] < LEADING)
        def _():
            out[...] = jnp.zeros_like(out)

        @pl.when(c * out.shape[1] < LEADING)
        def _():
            out[:, :LEADING] = jnp.zeros((out.shape[0], LEADING), F32)


def on_device(front_entries, child_updates, off, cnt):
    fronts = lax.axis_size("front")
    rows = lax.axis_size("row")
    cols = lax.axis_size("col")
    own_rows, own_cols = front_entries.shape
    owned = own_rows // BLOCK
    per_front = owned * rows
    per_col = own_cols // BLOCK
    r = lax.axis_index("row")
    c = lax.axis_index("col")
    row_blocks = off.shape[1] // rows
    block = (BLOCK, BLOCK)

    lead = call(
        lead_columns_body, "lead_columns", shape(cols, *block), [SMEM, SMEM, VMEM], VMEM
    )(off, cnt, child_updates)
    lead = lax.all_to_all(lead, "col", split_axis=0, concat_axis=0, tiled=True)
    strips = [front_entries[:, k * BLOCK : (k + 1) * BLOCK] for k in range(LEAD)]
    strip = jnp.where(c == 0, strips[0], 0.0)
    for k in range(1, cols):
        strip = strip + lax.ppermute(strips[k], "col", [(0, k)])
    top = jnp.where(lax.axis_index("front") == 0, strip, 0.0)
    for k in range(1, fronts):
        top = top + lax.ppermute(strip, "front", [(0, k)])
    corner, panel = call(
        functools.partial(lead_rows_body, per_front),
        "lead_rows",
        (shape(fronts, 2, *block), shape(fronts, 2, *block)),
        [SMEM, SMEM, VMEM],
        (VMEM, VMEM),
    )(off, cnt, lead)

    corner = lax.all_to_all(corner, "front", split_axis=0, concat_axis=0, tiled=True)
    piece = call(
        functools.partial(gather_rows_body, per_front, True),
        "corner_piece",
        shape(own_rows, BLOCK),
        [SMEM, SMEM, VMEM, VMEM],
        VMEM,
    )(off, cnt, corner, top)
    near = lax.ppermute(piece, "row", [(0, 1), (1, 0)])
    side = lax.ppermute(piece, "row", [(0, 3), (1, 2)])
    far = lax.ppermute(piece, "row", [(0, 2), (1, 3)])
    upper = jnp.where(r == 0, piece, jnp.where(r == 1, near, jnp.where(r == 2, far, side)))
    lower = jnp.where(r == 1, piece, jnp.where(r == 0, near, jnp.where(r == 2, side, far)))
    corner = lax.all_gather(jnp.concatenate([upper, lower], axis=0), "col", axis=0)
    u, inv = call(
        factor_body,
        "factor",
        (shape(LEADING, LEADING), shape(LEADING, BLOCK)),
        [VMEM],
        (VMEM, VMEM),
        [pltpu.VMEM((LEADING, LEADING), F32), pltpu.VMEM((BLOCK, 2 * BLOCK), F32)],
        flops=40 * 1150 * 10**6,
    )(corner)

    panel = lax.all_to_all(panel, "front", split_axis=0, concat_axis=0, tiled=True)
    strip = call(
        functools.partial(gather_rows_body, per_front, False),
        "panel_piece",
        shape(own_rows, BLOCK),
        [SMEM, SMEM, VMEM, VMEM],
        VMEM,
    )(off, cnt, panel, strip)
    mine = lax.all_gather(strip, "col", axis=0)
    swap = [
        ((i * rows + j) * cols + k, (k * rows + j) * cols + i)
        for i in range(fronts)
        for j in range(rows)
        for k in range(cols)
    ]
    across = lax.ppermute(strip, ("front", "row", "col"), swap)
    across = lax.all_gather(across, ("front", "row"), axis=0)
    across = across.reshape(LEAD, own_cols, BLOCK)
    m, t = call(
        solve_body,
        "solve",
        (shape(own_rows, LEADING), shape(own_rows, LEADING)),
        [VMEM, VMEM, VMEM],
        (VMEM, VMEM),
        [pltpu.VMEM((own_rows, LEADING), F32)],
        flops=12 * 1150 * 10**6,
    )(u, inv, mine)

    slots = 2 * rows
    rest = call(
        functools.partial(far_columns_body, per_col),
        "far_columns",
        shape(cols, slots, *block),
        [SMEM, SMEM, ANY],
        ANY,
        [pltpu.SemaphoreType.DMA((off.shape[1],)), pltpu.SMEM((cols,), jnp.int32)],
        moved=4 << 20,
    )(off, cnt, child_updates)
    rest = lax.all_to_all(rest, "col", split_axis=0, concat_axis=0, tiled=True)
    rest = call(
        functools.partial(far_rows_body, per_front),
        "far_rows",
        shape(fronts, 2, slots, *block),
        [SMEM, SMEM, ANY],
        ANY,
        [pltpu.SemaphoreType.DMA((row_blocks,))],
        moved=8 << 20,
    )(off, cnt, rest)
    rest = lax.all_to_all(rest, "front", split_axis=0, concat_axis=0, tiled=True)
    trailing = pl.pallas_call(
        functools.partial(final_body, per_front, per_col),
        name="final",
        grid=(LEAD // 2,),
        out_shape=shape(own_rows, own_cols),
        in_specs=[
            SMEM,
            SMEM,
            pl.BlockSpec((own_rows, LEADING), lambda i: (0, 0)),
            pl.BlockSpec((2, own_cols, BLOCK), lambda i: (i, 0, 0)),
            pl.BlockSpec((2, 2, slots, *block), lambda i: (i, 0, 0, 0, 0)),
            pl.BlockSpec((own_rows, own_cols), lambda i: (0, 0)),
        ],
        out_specs=pl.BlockSpec((own_rows, own_cols), lambda i: (0, 0)),
        compiler_params=pltpu.CompilerParams(vmem_limit_bytes=56 << 20),
        cost_estimate=pl.CostEstimate(
            flops=12 * 1150 * 10**6, bytes_accessed=24 << 20, transcendentals=0
        ),
    )(off, cnt, t, across, rest, front_entries)
    return trailing, m


def solution(mesh):
    placed = (P(("front", "row"), "col"), P("front", ("row", "col"), None), P(), P())
    return jax.shard_map(
        on_device,
        mesh=mesh,
        in_specs=placed,
        out_specs=(P(("front", "row"), "col"), P(("front", "row"), None)),
        check_vma=False,
    )
```

time: 1460 us -> 568 us (0.39)
  waiting for transfers between devices: 976 us -> 202 us
  other arithmetic: 274 us -> 4.1 us
  Pallas kernels: 0 us -> 217 us
  matrix products: 77.4 us -> 0 us
  local copies, waits for them, and re-layouts: 89.1 us -> 14.3 us
  starting transfers between devices: 14.4 us -> 75.3 us
  blocking collectives: 0 us -> 36.7 us
    psum x6 -> x0, waiting for transfers between devices: 750 us -> none  [spread(): return lax.psum(jnp.where(mine, x, jnp.zeros_like(x)), axis)]
    another operation x35 -> x0, other arithmetic: 241 us -> none  [the longest x30 159 us: on_device(): factor = jnp.linalg.cholesky(diagonal)]
    pallas_call x0 -> x9, Pallas kernels: none -> 217 us  [the longest x1 113 us: on_device(): call(functools.partial(far_rows_body, per_front), 'far_rows', shape(front...]
    all_to_all x2 -> x3, waiting for transfers between devices: 225 us -> 166 us  [the longest x1 109 us: on_device(): lax.all_to_all(rest, 'front', split_axis=0, concat_axis=0, tiled=True)]
    dot_general x6 -> x0, matrix products: 58.5 us -> none  [the longest x1 22.3 us: on_device(): jnp.einsum('gcs,gcxkb->gsxkb', row_select, arrived, precision=HIGHEST)]
    all_to_all x0 -> x2, blocking collectives: none -> 36.7 us  [the longest x1 22.2 us: on_device(): lax.all_to_all(panel, 'front', split_axis=0, concat_axis=0, tiled=True)]
    ppermute x0 -> x18, waiting for transfers between devices: none -> 35 us  [the longest x7 19.6 us: on_device(): top = top + lax.ppermute(strip, 'front', [(0, k)])]
    all_to_all x2 -> x3, starting transfers between devices: 13.3 us -> 45.3 us  [the longest x1 23.2 us: on_device(): lax.all_to_all(rest, 'front', split_axis=0, concat_axis=0, tiled=True)]
  transfers between devices with their start and end apart: 8 -> 24, of which waited for: 8 -> 8; matrix products, arithmetic and copies ran while one was open for 1% -> 1% of each run, Pallas kernels for 0% -> 33%
where the time goes in v1:
time: 568 us; the launch traced here: 563 us
  Pallas kernels  217 us (38%)
  waiting for transfers between devices  202 us (36%)
  starting transfers between devices  75.3 us (13%)
  blocking collectives  36.7 us (6%)
  between operations  14.5 us (3%)
  local copies, waits for them, and re-layouts  14.3 us (3%)
    pallas_call x1, Pallas kernels, on_device(): call(functools.partial(far_rows_body, per_front), 'far_rows', shape(front...  113 us
    all_to_all x1, waiting for transfers between devices, on_device(): lax.all_to_all(rest, 'front', split_axis=0, concat_axis=0, tiled=True)  109 us
    all_to_all x1, waiting for transfers between devices, on_device(): rest = lax.all_to_all(rest, 'col', split_axis=0, concat_axis=0, tiled=True)  57.3 us
    pallas_call x1, Pallas kernels, on_device(): call(factor_body, 'factor', (shape(LEADING, LEADING), shape(LEADING, BLOC...  42.2 us
    pallas_call x1, Pallas kernels, on_device(): call(solve_body, 'solve', (shape(own_rows, LEADING), shape(own_rows, LEAD...  28.1 us
    pallas_call x1, Pallas kernels, on_device(): pl.pallas_call(functools.partial(final_body, per_front, per_col), name='f...  23.8 us
    all_to_all x1, starting transfers between devices, on_device(): lax.all_to_all(rest, 'front', split_axis=0, concat_axis=0, tiled=True)  23.2 us
    all_to_all x1, blocking collectives, on_device(): lax.all_to_all(panel, 'front', split_axis=0, concat_axis=0, tiled=True)  22.2 us
  transfers between devices with their start and end apart: 24, of which 8 were waited for; matrix products, arithmetic and copies ran while one was open for 1% of the time, Pallas kernels for 33%

profile of v1, /device:TPU:32, one launch (start us, length us, event | category | flops | bytes accessed | tf_op | source)
XLA Modules:
  0.0 563.0 jit_solution(15677284530521773273)
XLA Ops:
  7.2 1.6 copy-done
  8.8 0.7 copy-done.6
  10.1 1.0 lead_columns.1
  11.1 14.5 %all_to_all.25.got = f32[8,128,128]{2,1,0:T(8,128)S(1)} all-to-all(f32[8,128,128]{2,1,0:T(8,128)S(1)} %lead_columns.1), channel_id=1, replica_groups=mesh['front'=8,'row'=4,'col'=8] {'col'}, dimensions={0} | all-to-all | bytes 1048576 | tf_op jit(solution)/shard_map/all_to_all | solution.py:354
  25.6 0.7 copy-done.7
  26.9 2.0 lead_rows.1
  28.9 1.0 copy-done.2
  29.9 8.6 %all-to-all-start.1 = ((f32[8,2,128,128]{3,2,1,0:T(8,128)}), f32[8,2,128,128]{3,2,1,0:T(8,128)S(1)}, u32[]{:S(2)}, u32[]{:S(2)}) async-start(f32[8,2,128,128]{3,2,1,0:T(8,128)} %get-tuple-element.8), calls=%async_computation.1 | async-start | bytes 2097152 | tf_op jit(solution)/shard_map/all_to_all | solution.py:370
  38.5 1.6 fusion
  40.1 1.3 collective-permute-start
  41.4 2.5 collective-permute-start.5
  43.9 1.3 collective-permute-start.4
  45.2 1.3 collective-permute-start.3
  46.5 2.0 collective-permute-start.2
  48.5 2.0 collective-permute-start.1
  50.5 2.0 collective-permute-start.6
  52.5 2.2 collective-permute-done.2
  54.7 2.8 collective-permute-done.1
  57.5 1.3 add_add_fusion.1.base
  63.0 1.3 collective-permute-start.7
  64.3 19.5 %collective-permute-done.7 = f32[512,128]{1,0:T(8,128)S(1)} collective-permute-done((f32[512,128]{1,0:T(8,128)S(1)}, f32[512,128]{1,0:T(8,128)S(1)}, u32[]{:S(2)}, u32[]{:S(2)}) %collective-permute-start.7) | collective-permute-done | bytes 262176 | tf_op jit(solution)/shard_map/ppermute | solution.py:361
  83.9 0.8 add_add_fusion.base
  84.7 1.1 copy-done.3
  85.8 2.6 corner_piece.1
  88.3 4.9 collective-permute-start.16
  93.2 1.5 collective-permute-start.15
  94.7 2.5 collective-permute-start.14
  97.3 2.9 collective-permute-done.16
  100.2 3.1 collective-permute-done.14
  103.3 1.1 select_select_fusion.1
  104.4 0.8 pad_maximum_fusion
  105.3 22.2 %all_to_all.26.got = f32[8,2,128,128]{3,2,1,0:T(8,128)S(1)} all-to-all(f32[8,2,128,128]{3,2,1,0:T(8,128)} %copy-done.2), channel_id=1, replica_groups=mesh['front'=8,'row'=4,'col'=8] {'front'}, dimensions={0} | all-to-all | bytes 2097152 | tf_op jit(solution)/shard_map/all_to_all | solution.py:394
  127.6 1.9 panel_piece.1
  130.2 2.1 far_columns.1
  132.3 13.6 %all-to-all-start.3 = ((f32[8,8,128,128]{3,2,1,0:T(8,128)}), f32[8,8,128,128]{3,2,1,0:T(8,128)}, u32[]{:S(2)}, u32[]{:S(2)}) async-start(f32[8,8,128,128]{3,2,1,0:T(8,128)} %far_columns.1), calls=%async_computation.3 | async-start | bytes 8388608 | tf_op jit(solution)/shard_map/all_to_all | solution.py:432
  146.0 3.3 collective-permute-start.17
  149.3 4.4 collective-permute-done.17
  153.6 0.7 copy-done.15
  154.4 57.3 %all-to-all-done.3.got = f32[8,8,128,128]{3,2,1,0:T(8,128)} async-done(((f32[8,8,128,128]{3,2,1,0:T(8,128)}), f32[8,8,128,128]{3,2,1,0:T(8,128)}, u32[]{:S(2)}, u32[]{:S(2)}) %all-to-all-start.3) | async-done | bytes 4194336 | tf_op jit(solution)/shard_map/all_to_all | solution.py:432
  211.7 113.0 %far_rows.1 = f32[8,2,8,128,128]{4,3,2,1,0:T(8,128)} custom-call(s32[8,32]{1,0:T(8,128)S(1)} %copy-done.8, s32[8]{0:T(128)S(1)} %copy-done.11, f32[8,8,128,128]{3,2,1,0:T(8,128)} %all-to-all-done.3.got), custom_call_target="tpu_custom_call" | custom-call | bytes 8388608 | tf_op jit(solution)/shard_map/far_rows/pallas_call | solution.py:433
  324.7 23.2 %all-to-all-start.4 = ((f32[8,2,8,128,128]{4,3,2,1,0:T(8,128)}), f32[8,2,8,128,128]{4,3,2,1,0:T(8,128)}, u32[]{:S(2)}, u32[]{:S(2)}) async-start(f32[8,2,8,128,128]{4,3,2,1,0:T(8,128)} %far_rows.1), calls=%async_computation.4 | async-start | bytes 16777216 | tf_op jit(solution)/shard_map/all_to_all | solution.py:442
  347.9 42.2 %factor.1 = (f32[1024,1024]{1,0:T(8,128)S(1)}, f32[1024,128]{1,0:T(8,128)S(1)}) custom-call(f32[8,1024,128]{2,1,0:T(8,128)} %bitcast.5), custom_call_target="tpu_custom_call" | custom-call | flops 46000001024 | tf_op jit(solution)/shard_map/factor/pallas_call | solution.py:384
  390.1 2.0 copy-done.14
  392.1 1.6 copy-done.12
  393.7 28.1 %solve.1 = (f32[512,1024]{1,0:T(8,128)}, f32[512,1024]{1,0:T(8,128)S(1)}) custom-call(f32[1024,1024]{1,0:T(8,128)} %copy-done.14, f32[1024,128]{1,0:T(8,128)S(1)} %get-tuple-element.10.inv, f32[8,512,128]{2,1,0:T(8,128)S(1)} %bitcast.3), custom_call_target="tpu_custom_call" | custom-call | flops 13799999488 | tf_op jit(solution)/shard_map/solve/pallas_call | solution.py:412
  421.8 1.3 copy-done.13
  423.1 109.1 %all-to-all-done.4.got = f32[8,2,8,128,128]{4,3,2,1,0:T(8,128)} async-done(((f32[8,2,8,128,128]{4,3,2,1,0:T(8,128)}), f32[8,2,8,128,128]{4,3,2,1,0:T(8,128)}, u32[]{:S(2)}, u32[]{:S(2)}) %all-to-all-start.4) | async-done | bytes 8388640 | tf_op jit(solution)/shard_map/all_to_all | solution.py:442
  532.3 23.8 %final.1 = f32[512,2048]{1,0:T(8,128)} custom-call(s32[8,32]{1,0:T(8,128)} %off.13, s32[8]{0:T(128)} %cnt.13, f32[512,1024]{1,0:T(8,128)} %copy-done.13, f32[8,2048,128]{2,1,0:T(8,128)} %bitcast.4, f32[8,2,8,128,128]{4,3,2,1,0:T(8,128)} %all-to-all-done.4.got, f32[512,2048]{1,0:T(8,128)} %base.1), custom_call_target="tpu_custom_call" | custom-call | flops 13799999488 | bytes 25165824 | tf_op jit(solution)/shard_map/final/pallas_call | solution.py:443
  (51 shorter events, 6.3 us)
Async XLA Ops:
  7.2 1.6 copy-start
  8.8 0.7 copy-start.6
  9.4 0.7 copy-start.9
  25.6 0.7 copy-start.7
  26.3 0.7 copy-start.10
  28.9 1.0 copy-start.2
  29.9 54.8 %all-to-all-start.1 = ((f32[8,2,128,128]{3,2,1,0:T(8,128)}), f32[8,2,128,128]{3,2,1,0:T(8,128)S(1)}, u32[]{:S(2)}, u32[]{:S(2)}) async-start(f32[8,2,128,128]{3,2,1,0:T(8,128)} %get-tuple-element.8), calls=%async_computation.1 | async-start | bytes 2097152 | tf_op jit(solution)/shard_map/all_to_all | solution.py:370
  38.5 46.2 %copy-start.8 = (s32[8,32]{1,0:T(8,128)S(1)}, s32[8,32]{1,0:T(8,128)}, u32[]{:S(2)}) copy-start(s32[8,32]{1,0:T(8,128)} %off.13) | copy-start | bytes 3076
  38.5 46.2 %copy-start.11 = (s32[8]{0:T(128)S(1)}, s32[8]{0:T(128)}, u32[]{:S(2)}) copy-start(s32[8]{0:T(128)} %cnt.13) | copy-start | bytes 100
  38.5 309.4 %all-gather.7.cloned.1.call-start = ((), (), s32[]{:S(2)}) async-start(), calls=%async_computation.5 | async-start | bytes 4718592 | tf_op jit(solution)/shard_map/all_gather | solution.py:383
  40.1 8.4 %collective-permute-start = (f32[512,128]{1,0:T(8,128)S(1)}, f32[512,128]{1,0:T(8,128)S(1)}, u32[]{:S(2)}, u32[]{:S(2)}) collective-permute-start(f32[512,128]{1,0:T(8,128)S(1)} %get-tuple-element.14), channel_id=1, source_target_pairs={{0,1},{8,9},{16,17},{24,25},{32,33},{40,41},{48,49},{56,57},{64,65... | collective-permute-start | bytes 786440 | tf_op jit(solution)/shard_map/ppermute | solution.py:358
  41.4 9.1 %collective-permute-start.5 = (f32[512,128]{1,0:T(8,128)S(1)}, f32[512,128]{1,0:T(8,128)S(1)}, u32[]{:S(2)}, u32[]{:S(2)}) collective-permute-start(f32[512,128]{1,0:T(8,128)S(1)} %get-tuple-element.15), channel_id=1, source_target_pairs={{0,6},{8,14},{16,22},{24,30},{32,38},{40,46},{48,54},{56,62},{64,7... | collective-permute-start | bytes 786440 | tf_op jit(solution)/shard_map/ppermute | solution.py:358
  43.9 8.6 %collective-permute-start.4 = (f32[512,128]{1,0:T(8,128)S(1)}, f32[512,128]{1,0:T(8,128)S(1)}, u32[]{:S(2)}, u32[]{:S(2)}) collective-permute-start(f32[512,128]{1,0:T(8,128)S(1)} %get-tuple-element.16), channel_id=1, source_target_pairs={{0,5},{8,13},{16,21},{24,29},{32,37},{40,45},{48,53},{56,61},{64,6... | collective-permute-start | bytes 786440 | tf_op jit(solution)/shard_map/ppermute | solution.py:358
  45.2 7.3 %collective-permute-start.3 = (f32[512,128]{1,0:T(8,128)S(1)}, f32[512,128]{1,0:T(8,128)S(1)}, u32[]{:S(2)}, u32[]{:S(2)}) collective-permute-start(f32[512,128]{1,0:T(8,128)S(1)} %get-tuple-element.17), channel_id=1, source_target_pairs={{0,4},{8,12},{16,20},{24,28},{32,36},{40,44},{48,52},{56,60},{64,6... | collective-permute-start | bytes 786440 | tf_op jit(solution)/shard_map/ppermute | solution.py:358
  46.5 8.2 %collective-permute-start.2 = (f32[512,128]{1,0:T(8,128)S(1)}, f32[512,128]{1,0:T(8,128)}, u32[]{:S(2)}, u32[]{:S(2)}) collective-permute-start(f32[512,128]{1,0:T(8,128)S(1)} %get-tuple-element.18), channel_id=1, source_target_pairs={{0,3},{8,11},{16,19},{24,27},{32,35},{40,43},{48,51},{56,59},{64,6... | collective-permute-start | bytes 786440 | tf_op jit(solution)/shard_map/ppermute | solution.py:358
  48.5 9.0 %collective-permute-start.1 = (f32[512,128]{1,0:T(8,128)S(1)}, f32[512,128]{1,0:T(8,128)}, u32[]{:S(2)}, u32[]{:S(2)}) collective-permute-start(f32[512,128]{1,0:T(8,128)S(1)} %get-tuple-element.19), channel_id=1, source_target_pairs={{0,2},{8,10},{16,18},{24,26},{32,34},{40,42},{48,50},{56,58},{64,6... | collective-permute-start | bytes 786440 | tf_op jit(solution)/shard_map/ppermute | solution.py:358
  50.5 7.0 %collective-permute-start.6 = (f32[512,128]{1,0:T(8,128)S(1)}, f32[512,128]{1,0:T(8,128)}, u32[]{:S(2)}, u32[]{:S(2)}) collective-permute-start(f32[512,128]{1,0:T(8,128)S(1)} %get-tuple-element.20), channel_id=1, source_target_pairs={{0,7},{8,15},{16,23},{24,31},{32,39},{40,47},{48,55},{56,63},{64,7... | collective-permute-start | bytes 786440 | tf_op jit(solution)/shard_map/ppermute | solution.py:358
  58.8 3.4 collective-permute-start.13
  59.5 3.4 collective-permute-start.12
  60.2 4.1 collective-permute-start.11
  60.9 3.4 collective-permute-start.10
  61.6 2.7 collective-permute-start.9
  62.3 2.0 collective-permute-start.8
  63.0 20.9 %collective-permute-start.7 = (f32[512,128]{1,0:T(8,128)S(1)}, f32[512,128]{1,0:T(8,128)S(1)}, u32[]{:S(2)}, u32[]{:S(2)}) collective-permute-start(f32[512,128]{1,0:T(8,128)S(1)} %add_add_fusion.1.base), channel_id=1, source_target_pairs={{0,32},{1,33},{2,34},{3,35},{4,36},{5,37},{6,38},{7,39},{8,40},{9,... | collective-permute-start | bytes 786440 | tf_op jit(solution)/shard_map/ppermute | solution.py:361
  84.7 45.5 %copy-start.1 = (f32[1,128,4096]{2,1,0:T(8,128)S(1)}, f32[1,128,4096]{2,1,0:T(8,128)}, u32[]{:S(2)}) copy-start(f32[1,128,4096]{2,1,0:T(8,128)} %child.3) | copy-start | bytes 6291460
  84.7 1.1 copy-start.3
  88.3 11.9 %collective-permute-start.16 = (f32[512,128]{1,0:T(8,128)}, f32[512,128]{1,0:T(8,128)S(1)}, u32[]{:S(2)}, u32[]{:S(2)}) collective-permute-start(f32[512,128]{1,0:T(8,128)} %corner_piece.1), channel_id=1, source_target_pairs={{0,24},{8,16},{1,25},{9,17},{2,26},{10,18},{3,27},{11,19},{4,28},{... | collective-permute-start | bytes 786440 | tf_op jit(solution)/shard_map/ppermute | solution.py:379
  93.2 7.0 %collective-permute-start.15 = (f32[512,128]{1,0:T(8,128)}, f32[512,128]{1,0:T(8,128)S(1)}, u32[]{:S(2)}, u32[]{:S(2)}) collective-permute-start(f32[512,128]{1,0:T(8,128)} %corner_piece.1), channel_id=1, source_target_pairs={{0,16},{8,24},{1,17},{9,25},{2,18},{10,26},{3,19},{11,27},{4,20},{... | collective-permute-start | bytes 786440 | tf_op jit(solution)/shard_map/ppermute | solution.py:380
  94.7 8.6 %collective-permute-start.14 = (f32[512,128]{1,0:T(8,128)}, f32[512,128]{1,0:T(8,128)}, u32[]{:S(2)}, u32[]{:S(2)}) collective-permute-start(f32[512,128]{1,0:T(8,128)} %corner_piece.1), channel_id=1, source_target_pairs={{0,8},{8,0},{1,9},{9,1},{2,10},{10,2},{3,11},{11,3},{4,12},{12,4},... | collective-permute-start | bytes 786440 | tf_op jit(solution)/shard_map/ppermute | solution.py:378
  105.3 286.8 %all-gather.9.cloned.1.call-start = ((), (), s32[]{:S(2)}) async-start(), calls=%async_computation.6 | async-start | bytes 2359296 | tf_op jit(solution)/shard_map/all_gather | solution.py:402
  129.5 0.7 copy-start.4
  132.3 13.6 %copy-start.5 = (f32[512,128]{1,0:T(8,128)S(1)}, f32[512,128]{1,0:T(8,128)}, u32[]{:S(2)}) copy-start(f32[512,128]{1,0:T(8,128)} %copy-done.4) | copy-start | bytes 786436
  132.3 79.4 %all-to-all-start.3 = ((f32[8,8,128,128]{3,2,1,0:T(8,128)}), f32[8,8,128,128]{3,2,1,0:T(8,128)}, u32[]{:S(2)}, u32[]{:S(2)}) async-start(f32[8,8,128,128]{3,2,1,0:T(8,128)} %far_columns.1), calls=%async_computation.3 | async-start | bytes 8388608 | tf_op jit(solution)/shard_map/all_to_all | solution.py:432
  145.9 386.4 %all-gather.11.cloned.1.call-start = ((), (), s32[]{:S(2)}) async-start(), calls=%async_computation.7 | async-start | bytes 8650752 | tf_op jit(solution)/shard_map/all_gather | solution.py:410
  146.0 7.7 %collective-permute-start.17 = (f32[512,128]{1,0:T(8,128)S(1)}, f32[512,128]{1,0:T(8,128)S(1)}, u32[]{:S(2)}, u32[]{:S(2)}) collective-permute-start(f32[512,128]{1,0:T(8,128)S(1)} %copy-done.5), channel_id=1, source_target_pairs={{0,0},{1,32},{2,64},{3,96},{4,128},{5,160},{6,192},{7,224},{8,8},{... | collective-permute-start | bytes 786440 | tf_op jit(solution)/shard_map/ppermute | solution.py:409
  153.6 0.7 copy-start.15
  324.7 207.6 %all-to-all-start.4 = ((f32[8,2,8,128,128]{4,3,2,1,0:T(8,128)}), f32[8,2,8,128,128]{4,3,2,1,0:T(8,128)}, u32[]{:S(2)}, u32[]{:S(2)}) async-start(f32[8,2,8,128,128]{4,3,2,1,0:T(8,128)} %far_rows.1), calls=%async_computation.4 | async-start | bytes 16777216 | tf_op jit(solution)/shard_map/all_to_all | solution.py:442
  390.1 2.0 copy-start.14
  392.1 1.6 copy-start.12
  421.8 1.3 copy-start.13
Sparse Core Ops, SparseCore 0:
  105.4 34.9 all-gather.6
  142.3 40.4 all-gather.8
  185.3 97.5 all-gather.10
